TPU v7x, 512 devices: a whole 4x4x16 slice. The times are simulated.
512 devices in a mesh: role: 8 (over z_lo, core), fsdp: 64 (over z_hi, y, x).
Axes of the slice: x: 4, y: 4, z: 16 (z_hi: 4, z_lo: 4; z = z_hi * 4 + z_lo), core: 2. Of those that a mesh axis runs over, the one named last changes fastest.
Arguments:
- teacher_hidden: bfloat16 [8192, 16384], P('fsdp', 'role'), may hold values from -28 to 28
- teacher_head: bfloat16 [16384, 2048], P(('role', 'fsdp')), may hold values from -0.25 to 0.25
- student_hidden: bfloat16 [8192, 4096], P('fsdp', 'role'), may hold values from -28 to 28
- student_head: bfloat16 [4096, 2048], P(('role', 'fsdp')), may hold values from -0.5 to 0.5
- teacher_rest: float32 [8192], P('fsdp'), may hold values from 6 to 14
- student_rest: float32 [8192], P('fsdp'), may hold values from 6 to 14
Outputs:
- kl_loss: float32 [8192], P('fsdp')
- grad_head: float32 [4096, 2048], P(('role', 'fsdp'))
- grad_hidden: float32 [8192, 4096], P('fsdp', 'role')
All inputs are finite; a program needn't handle non-finite values.
Results may differ from a plain program's by a relative error of at most 0.003.
Values may be sent and summed in bfloat16 or wider, within the bound.
A program may use at most 64 MiB of HBM per device.

v0:
```python
import jax
import jax.numpy as jnp
from jax import lax
from jax.sharding import PartitionSpec as P


def log_normalize(scaled, rest):
    top = jnp.max(scaled, axis=-1, keepdims=True)
    local = top + jnp.log(jnp.sum(jnp.exp(scaled - top), axis=-1, keepdims=True))
    return scaled - jnp.logaddexp(local, rest[:, None])


def distill(teacher_logits, student_logits, teacher_rest, student_rest):
    log_teacher = log_normalize(teacher_logits / 2.0, teacher_rest)
    log_student = log_normalize(student_logits / 2.0, student_rest)
    prob_teacher = jnp.exp(log_teacher)
    prob_student = jnp.exp(log_student)
    kl_loss = 16.0 * jnp.sum(prob_teacher * (log_teacher - log_student), axis=-1)
    grad_logits = (8.0 * (prob_student - prob_teacher)).astype(jnp.bfloat16)
    return (kl_loss, grad_logits)


def body(teacher_hidden, teacher_head, student_hidden, student_head, teacher_rest, student_rest):
    columns = teacher_hidden
    teacher_part = jnp.dot(
        columns,
        lax.all_gather(teacher_head, "fsdp", axis=0, tiled=True),
        preferred_element_type=jnp.float32,
    )
    student_block = lax.all_gather(student_head, "fsdp", axis=0, tiled=True)
    student_part = jnp.dot(student_hidden, student_block, preferred_element_type=jnp.float32)
    teacher_logits, student_logits = lax.psum((teacher_part, student_part), "role")
    kl_loss, grad_logits = distill(teacher_logits, student_logits, teacher_rest, student_rest)
    columns = student_hidden
    grad_head = lax.psum_scatter(
        lax.dot_general(
            columns, grad_logits, (((0,), (0,)), ((), ())), preferred_element_type=jnp.float32
        ),
        "fsdp",
        scatter_dimension=0,
        tiled=True,
    )
    grad_hidden = lax.dot_general(
        grad_logits, student_block, (((1,), (1,)), ((), ())), preferred_element_type=jnp.float32
    )
    return (kl_loss, grad_head, grad_hidden)


def solution(mesh):
    return jax.shard_map(
        body,
        mesh=mesh,
        in_specs=(
            P("fsdp", "role"),
            P(("role", "fsdp"), None),
            P("fsdp", "role"),
            P(("role", "fsdp"), None),
            P("fsdp"),
            P("fsdp"),
        ),
        out_specs=(P("fsdp"), P(("role", "fsdp"), None), P("fsdp", "role")),
        check_vma=False,
    )
```

profile of v0, /device:TPU:0, one launch (start us, length us, event | category | flops | bytes accessed | tf_op | source)
XLA Modules:
  0.0 892.2 jit_solution(4208810796679744950)
XLA Ops:
  7.2 0.0 copy-start
  7.2 0.0 all-gather.5.cloned.1.call-start
  7.2 0.7 all-gather.5.cloned.1.call-update
  7.9 0.0 all-gather.3.cloned.1.call-start
  8.0 0.7 all-gather.3.cloned.1.call-update
  8.7 0.0 all-reduce.3.cloned.1.call-start
  8.7 117.7 %all-gather.5.cloned.1.call-done = bf16[512,2048]{1,0:T(8,128)(2,1)} async-done(((bf16[8,2048]{1,0:T(8,128)(2,1)}), bf16[512,2048]{1,0:T(8,128)(2,1)}) %all-gather.5.cloned.1.call-update) | async-done | bytes 2097168 | tf_op jit(solution)/shard_map/all_gather | solution.py:30
  126.4 3.1 fusion.1
  129.5 188.9 %all-gather.3.cloned.1.call-done = bf16[2048,2048]{1,0:T(8,128)(2,1)} async-done(((bf16[32,2048]{1,0:T(8,128)(2,1)}), bf16[2048,2048]{1,0:T(8,128)(2,1)}) %all-gather.3.cloned.1.call-update) | async-done | bytes 8388624 | tf_op jit(solution)/shard_map/all_gather | solution.py:27
  318.4 0.0 copy-done
  318.4 5.6 fusion
  324.0 0.0 copy-start.5
  324.0 0.0 copy-start.6
  324.0 0.0 copy-start.4
  324.0 0.0 all-reduce.3.cloned.1.call-update
  324.0 0.0 reduce-scatter.4.cloned.1.call-start
  324.1 87.1 %all-reduce.3.cloned.1.call-done = (f32[128,2048]{1,0:T(8,128)}, f32[128,2048]{1,0:T(8,128)}) async-done(((f32[128,2048]{1,0:T(8,128)}, f32[128,2048]{1,0:T(8,128)}), (f32[128,2048]{1,0:T(8,128)}, f32[128,2048]{1,0:T(8,128)})) %all-reduce.3.cloned.1.call-update) | async-done | bytes 2097168 | tf_op jit(solution)/shard_map/psum | solution.py:32
  411.2 0.0 copy-start.1
  411.2 0.0 copy-start.2
  411.2 1.5 multiply_reduce_fusion.1
  412.7 1.4 multiply_reduce_fusion.2
  414.1 2.0 exponential_reduce_fusion
  416.1 0.0 copy-done.5
  416.2 0.0 copy-done.6
  416.2 0.0 copy-done.1
  416.2 0.0 copy-done.2
  416.2 0.6 multiply_convert_fusion
  416.8 0.0 copy-done.4
  416.8 2.7 convolution_bitcast_fusion
  419.5 5.4 copy.11
  424.9 0.0 copy-start.3
  424.9 0.0 reduce-scatter.4.cloned.1.call-update
  424.9 0.5 broadcast_multiply_fusion
  425.5 1.1 copy-done.3
  426.5 1.5 fusion.2
  428.1 457.6 %reduce-scatter.4.cloned.1.call-done = f32[8,2048]{1,0:T(8,128)} async-done(((f32[512,2048]{1,0:T(8,128)}), f32[8,2048]{1,0:T(8,128)}) %reduce-scatter.4.cloned.1.call-update) | async-done | bytes 65552
  (2 shorter events, 0.0 us)
Async XLA Ops:
  7.2 311.2 %copy-start = (bf16[128,2048]{1,0:T(8,128)(2,1)S(1)}, bf16[128,2048]{1,0:T(8,128)(2,1)}, u32[]{:S(2)}) copy-start(bf16[128,2048]{1,0:T(8,128)(2,1)} %param.6) | copy-start | bytes 1572868
  7.2 119.2 %all-gather.5.cloned.1.call-start = ((), (), s32[]{:S(2)}) async-start(), calls=%async_computation.2 | async-start | bytes 2129920 | tf_op jit(solution)/shard_map/all_gather | solution.py:30
  7.9 310.5 %all-gather.3.cloned.1.call-start = ((), (), s32[]{:S(2)}) async-start(), calls=%async_computation.1 | async-start | bytes 8519680 | tf_op jit(solution)/shard_map/all_gather | solution.py:27
  8.7 402.5 %all-reduce.3.cloned.1.call-start = ((), (), s32[]{:S(2)}) async-start(), calls=%async_computation.4 | async-start | bytes 4194304 | tf_op jit(solution)/shard_map/psum | solution.py:32
  324.0 92.1 %copy-start.5 = (f32[128]{0:T(128)S(1)}, f32[128]{0:T(128)}, u32[]{:S(2)}) copy-start(f32[128]{0:T(128)} %param.11) | copy-start | bytes 1540
  324.0 92.1 %copy-start.6 = (f32[128]{0:T(128)S(1)}, f32[128]{0:T(128)}, u32[]{:S(2)}) copy-start(f32[128]{0:T(128)} %param.10) | copy-start | bytes 1540
  324.0 92.8 %copy-start.4 = (bf16[128,512]{1,0:T(8,128)(2,1)S(1)}, bf16[128,512]{1,0:T(8,128)(2,1)}, u32[]{:S(2)}) copy-start(bf16[128,512]{1,0:T(8,128)(2,1)} %param.8) | copy-start | bytes 393220
  324.0 561.6 %reduce-scatter.4.cloned.1.call-start = ((), (), s32[]{:S(2)}) async-start(), calls=%async_computation.3 | async-start | bytes 4259840
  411.2 5.0 copy-start.1
  411.2 5.0 copy-start.2
  424.9 1.6 copy-start.3
Sparse Core Ops, SparseCore 0:
  12.2 114.1 all-gather.4
  130.6 187.7 all-gather.2
  324.2 86.9 all-reduce.2
  425.1 460.5 reduce-scatter.3
where the time goes:
time: 893 us; the launch traced here: 892 us
  waiting for transfers between devices  853 us (96%)
  between operations  13.8 us (2%)
  matrix products  12.9 us (1%)
    unnamed x5, waiting for transfers between devices  459 us
    all_gather x1, waiting for transfers between devices, body(): lax.all_gather(teacher_head, 'fsdp', axis=0, tiled=True)  189 us
    all_gather x1, waiting for transfers between devices, body(): student_block = lax.all_gather(student_head, 'fsdp', axis=0, tiled=True)  118 us
    psum x1, waiting for transfers between devices, body(): lax.psum((teacher_part, student_part), 'role')  87.1 us
  transfers between devices with their start and end apart: 4, of which 4 were waited for; matrix products, arithmetic and copies ran while one was open for 1% of the time, Pallas kernels for 0%

commit v1 on v0

v1 whole, which is shorter than its diff:
```python
import jax
import jax.numpy as jnp
from jax import lax
from jax.experimental import pallas as pl
from jax.experimental.pallas import tpu as pltpu
from jax.sharding import PartitionSpec as P

MESH = pl.DeviceIdType.MESH
F32 = jnp.float32
BF16 = jnp.bfloat16
N_COPY = 112


def mod4(v):
    return lax.rem(v + 8, 4)


def distill_kernel(
    at_hbm,
    bt_hbm,
    as_hbm,
    sh_ref,
    tr_ref,
    sr_ref,
    kl_out,
    gw_out,
    gh_out,
    bs_src,
    rest_src,
    at_buf,
    as_buf,
    bt_buf,
    bs_buf,
    bs_full,
    as_t,
    rest_buf,
    ct_send,
    ct_recv,
    ct_own,
    cs_send,
    cs_recv,
    cs_own,
    zt_recv,
    zs_recv,
    stat_buf,
    g_buf,
    kl_buf,
    gh_own,
    gh_send,
    gh_recv,
    gw_own,
    gw_send,
    gw_recv,
    w2_send,
    w2_recv,
    send_sem,
    recv_sem,
    local_sem,
):
    role = lax.axis_index("role")
    fsdp = lax.axis_index("fsdp")
    zl, c = lax.div(role, 2), lax.rem(role, 2)
    zh, y, x = lax.div(fsdp, 16), lax.rem(lax.div(fsdp, 4), 4), lax.rem(fsdp, 4)

    def dev(dzl=0, dc=0, dzh=0, dy=0, dx=0):
        r = mod4(zl + dzl) * 2 + lax.rem(c + dc, 2)
        f = (mod4(zh + dzh) * 4 + mod4(y + dy)) * 4 + mod4(x + dx)
        return (r, f)

    started = []

    def send(src, dst, to):
        k = len(started)
        copy = pltpu.make_async_remote_copy(
            src_ref=src,
            dst_ref=dst,
            send_sem=send_sem.at[k],
            recv_sem=recv_sem.at[k],
            device_id=to,
            device_id_type=MESH,
        )
        copy.start()
        started.append(copy)
        return copy

    def arrive(*copies):
        for copy in copies:
            copy.wait_recv()

    partners = [dev(dzh=a, dx=b) for a in range(4) for b in range(4) if a + b > 0]
    partners += [dev(dy=d) for d in (1, 2, 3)]
    partners += [dev(dzl=a, dc=b) for a in range(4) for b in range(2) if a + b > 0]
    barrier = pltpu.get_barrier_semaphore()
    for to in partners:
        pl.semaphore_signal(barrier, inc=1, device_id=to, device_id_type=MESH)

    own_at = pltpu.make_async_copy(at_hbm, at_buf.at[x], local_sem.at[0])
    own_as = pltpu.make_async_copy(as_hbm, as_buf.at[x], local_sem.at[1])
    piece = zh * 4 + y
    row32 = pl.multiple_of(x * 32, 32)
    row16 = pl.multiple_of(x * 16, 16)
    own_bt = pltpu.make_async_copy(
        bt_hbm.at[:, pl.ds(pl.multiple_of(x * 512, 512), 512)],
        bt_buf.at[piece, pl.ds(row32, 32)],
        local_sem.at[2],
    )
    own_as.start()
    own_bt.start()
    own_at.start()

    for q in range(4):
        wide = sh_ref[:, q * 512 : (q + 1) * 512].astype(F32)
        bs_src[q] = jnp.concatenate([wide[:, :256], wide[:, 256:]], axis=0).astype(BF16)
    bs_buf[piece, pl.ds(row16, 16)] = bs_src[x]
    r8 = lax.broadcasted_iota(jnp.int32, (8, 128), 0)
    rest = jnp.where(r8 == 0, tr_ref[...], jnp.where(r8 == 1, sr_ref[...], 0.0))
    rest_src[...] = rest
    rest_buf[x] = rest

    pl.semaphore_wait(barrier, len(partners))

    bs_a2a, bt_a2a = [], []
    for d in (1, 3, 2):
        q = mod4(x + d)
        bs_a2a.append(send(bs_src.at[q], bs_buf.at[piece, pl.ds(row16, 16)], dev(dx=d)))
    for d in (1, 3, 2):
        q = mod4(x + d)
        bt_a2a.append(
            send(
                bt_hbm.at[:, pl.ds(pl.multiple_of(q * 512, 512), 512)],
                bt_buf.at[piece, pl.ds(row32, 32)],
                dev(dx=d),
            )
        )
    as_1 = [send(as_hbm, as_buf.at[x], dev(dx=d)) for d in (1, 3)]
    rests = [send(rest_src, rest_buf.at[x], dev(dx=d)) for d in (1, 3, 2)]
    at_1 = [send(at_hbm, at_buf.at[x], dev(dx=d)) for d in (1, 3)]

    def halves(buf, i, rows):
        return buf.at[i, pl.ds(0, rows)], buf.at[i, pl.ds(rows, rows)]

    def forward_x(first, buf):
        arrive(first[0])
        lo = halves(buf, mod4(x - 1), 64)[0]
        a = send(lo, lo, dev(dx=1))
        arrive(first[1])
        hi = halves(buf, mod4(x + 1), 64)[1]
        b = send(hi, hi, dev(dx=3))
        return [a, b]

    def both_y(buf, i):
        return [send(buf.at[i], buf.at[i], dev(dy=d)) for d in (1, 3)]

    def both_z(buf):
        return [send(buf.at[piece], buf.at[piece], dev(dzh=d)) for d in (1, 3)]

    def forward_z(first, buf, rows):
        arrive(first[0])
        i = mod4(zh - 1) * 4 + y
        lo = halves(buf, i, rows)[0]
        a = send(lo, lo, dev(dzh=1))
        ya = both_y(buf, i)
        arrive(first[1])
        i = mod4(zh + 1) * 4 + y
        hi = halves(buf, i, rows)[1]
        b = send(hi, hi, dev(dzh=3))
        yb = both_y(buf, i)
        return [a, b], ya, yb

    def forward_y(first, buf, zi, rows):
        arrive(first[0])
        lo = halves(buf, zi * 4 + mod4(y - 1), rows)[0]
        a = send(lo, lo, dev(dy=1))
        arrive(first[1])
        hi = halves(buf, zi * 4 + mod4(y + 1), rows)[1]
        b = send(hi, hi, dev(dy=3))
        return [a, b]

    prev, nxt, far = mod4(zh - 1), mod4(zh + 1), mod4(zh + 2)

    arrive(*bs_a2a)
    bs_z = both_z(bs_buf)
    bs_y0 = both_y(bs_buf, piece)
    own_bt.wait()
    arrive(*bt_a2a)
    bt_z = both_z(bt_buf)
    bt_y0 = both_y(bt_buf, piece)

    as_2 = forward_x(as_1, as_buf)
    bs_z2, bs_y1, bs_y2 = forward_z(bs_z, bs_buf, 32)
    bs_f0 = forward_y(bs_y0, bs_buf, zh, 32)
    bt_f0 = forward_y(bt_y0, bt_buf, zh, 64)
    bs_f1 = forward_y(bs_y1, bs_buf, prev, 32)
    bs_f2 = forward_y(bs_y2, bs_buf, nxt, 32)
    arrive(*bs_z2)
    bs_y3 = both_y(bs_buf, far * 4 + y)

    own_as.wait()
    arrive(*as_2)

    def turn(i, carry):
        cols = pl.ds(pl.multiple_of(i * 128, 128), 128)
        block = as_buf[:, :, cols].reshape(512, 128).astype(F32)
        flat = block.T.astype(BF16)
        for yy in range(4):
            at = pl.multiple_of((yy * 4 + i) * 32, 32)
            as_t[pl.ds(at, 32)] = flat[yy * 32 : (yy + 1) * 32]
        return carry

    lax.fori_loop(0, 4, turn, 0)

    bs_f3 = forward_y(bs_y3, bs_buf, far, 32)
    arrive(*bs_f0, *bs_f1, *bs_f2, *bs_f3)
    for i in range(16):
        tall = bs_buf[i].astype(F32).reshape(4, 2, 8, 256)
        rows = slice(i * 32, (i + 1) * 32)
        bs_full[rows, :256] = tall[:, 0].reshape(32, 256).astype(BF16)
        bs_full[rows, 256:] = tall[:, 1].reshape(32, 256).astype(BF16)

    def logits(a_buf, b_of, out, half):
        a = a_buf[pl.ds(half * 2, 2)]
        a = a.reshape(256, a.shape[-1])

        def column(i, carry):
            cols = pl.ds(pl.multiple_of(i * 256, 256), 256)
            out[:, cols] = jnp.dot(a, b_of(cols), preferred_element_type=F32)
            return carry

        lax.fori_loop(0, 2, column, 0)

    def student_b(cols):
        return bs_full[:, cols]

    logits(as_buf, student_b, cs_send, 1 - c)
    cs_swap = send(cs_send, cs_recv, dev(dc=1))
    logits(as_buf, student_b, cs_own, c)

    at_2 = forward_x(at_1, at_buf)
    bt_z2, bt_y1, bt_y2 = forward_z(bt_z, bt_buf, 64)
    bt_f1 = forward_y(bt_y1, bt_buf, prev, 64)
    bt_f2 = forward_y(bt_y2, bt_buf, nxt, 64)
    arrive(*bt_z2)
    bt_y3 = both_y(bt_buf, far * 4 + y)

    def scatter_z(swap, own, recv, zrecv):
        arrive(swap)
        own[...] = own[...] + recv[...]
        copies = []
        for d in (1, 3, 2):
            rows = pl.ds(pl.multiple_of(mod4(zl + d) * 64, 64), 64)
            copies.append(send(own.at[rows], zrecv.at[d - 1], dev(dzl=d)))
        return copies

    cs_z = scatter_z(cs_swap, cs_own, cs_recv, zs_recv)
    bt_f3 = forward_y(bt_y3, bt_buf, far, 64)
    arrive(*bt_f0, *bt_f1, *bt_f2, *bt_f3)
    own_at.wait()
    arrive(*at_2)

    def teacher_b(cols):
        return bt_buf[:, :, cols].reshape(2048, 256)

    logits(at_buf, teacher_b, ct_send, 1 - c)
    ct_swap = send(ct_send, ct_recv, dev(dc=1))
    logits(at_buf, teacher_b, ct_own, c)
    ct_z = scatter_z(ct_swap, ct_own, ct_recv, zt_recv)

    mine = pl.ds(pl.multiple_of(zl * 64, 64), 64)

    def scaled(own, zrecv):
        return (own[mine] + zrecv[0] + zrecv[1] + zrecv[2]) * 0.5

    arrive(*cs_z)
    s = scaled(cs_own, zs_recv)
    ms = jnp.max(s, axis=-1, keepdims=True)
    es = jnp.sum(jnp.exp(s - ms), axis=-1, keepdims=True)
    arrive(*ct_z)
    t = scaled(ct_own, zt_recv)
    mt = jnp.max(t, axis=-1, keepdims=True)
    et = jnp.exp(t - mt)
    ws = jnp.sum(et * (t - s), axis=-1, keepdims=True)
    et = jnp.sum(et, axis=-1, keepdims=True)

    lane = lax.broadcasted_iota(jnp.int32, (64, 128), 1)
    stat = jnp.zeros((64, 128), F32)
    for i, col in enumerate((mt, et, ms, es, ws)):
        stat = jnp.where(lane == i, col, stat)
    stat_buf[x] = stat
    stats = [send(stat_buf.at[x], stat_buf.at[x], dev(dx=d)) for d in (1, 3, 2)]

    arrive(*rests)
    rests8 = rest_buf[c * 2 + lax.div(zl, 2)]
    token = lax.broadcasted_iota(jnp.int32, (64, 128), 0) + lax.rem(zl, 2) * 64
    hit = token == lane
    rest_t = jnp.sum(jnp.where(hit, rests8[0:1], 0.0), axis=-1, keepdims=True)
    rest_s = jnp.sum(jnp.where(hit, rests8[1:2], 0.0), axis=-1, keepdims=True)

    arrive(*stats)
    got = [stat_buf[i] for i in range(4)]

    def log_add(a, b):
        top = jnp.maximum(a, b)
        return top + jnp.log(jnp.exp(a - top) + jnp.exp(b - top))

    def whole(k):
        tops = [v[:, k : k + 1] for v in got]
        sums = [v[:, k + 1 : k + 2] for v in got]
        top = jnp.maximum(jnp.maximum(tops[0], tops[1]), jnp.maximum(tops[2], tops[3]))
        scale = [jnp.exp(m - top) for m in tops]
        total = sum(a * b for a, b in zip(sums, scale))
        return top, scale, total

    top_t, scale_t, sum_t = whole(0)
    top_s, _, sum_s = whole(2)
    norm_t = log_add(top_t + jnp.log(sum_t), rest_t)
    norm_s = log_add(top_s + jnp.log(sum_s), rest_s)
    grad = (8.0 * (jnp.exp(s - norm_s) - jnp.exp(t - norm_t))).astype(BF16)
    j = c * 4 + zl
    g_buf[j] = grad
    g_chip = send(g_buf.at[j], g_buf.at[j], dev(dc=1))
    g_z = [send(g_buf.at[j], g_buf.at[j], dev(dzl=d)) for d in (1, 3, 2)]

    weighted = sum(v[:, 4:5] * b for v, b in zip(got, scale_t))
    inside = jnp.exp(top_t - norm_t)
    kl = 16.0 * (weighted * inside - sum_t * inside * (norm_t - norm_s))
    kl_row = jnp.sum(jnp.where(hit, kl, 0.0), axis=0, keepdims=True)
    kl_buf[j] = jnp.broadcast_to(kl_row, (8, 128))
    kls = [
        send(kl_buf.at[j], kl_buf.at[j], dev(dzl=a, dc=b))
        for a in range(4)
        for b in range(2)
        if a + b > 0
    ]

    g_f = []
    for copy, d in zip(g_z, (1, 3, 2)):
        arrive(copy)
        k = c * 4 + mod4(zl - d)
        g_f.append(send(g_buf.at[k], g_buf.at[k], dev(dc=1)))
    arrive(g_chip, *g_f)

    g = g_buf[...].reshape(512, 512)

    def head(i, carry):
        rows = pl.ds(pl.multiple_of(i * 128, 128), 128)
        part = jnp.dot(as_t[rows], g, preferred_element_type=F32)
        gw_send[i] = part.astype(BF16)

        @pl.when(i == y)
        def _():
            gw_own[...] = part

        return carry

    lax.fori_loop(0, 4, head, 0)
    gw_c = [
        send(gw_send.at[mod4(y + d)], gw_recv.at[d - 1], dev(dy=d)) for d in (1, 3, 2)
    ]

    def hidden(i, carry):
        rows = g_buf[pl.ds(i * 2, 2)].reshape(128, 512)
        part = lax.dot_general(
            rows, bs_full[...], (((1,), (1,)), ((), ())), preferred_element_type=F32
        )
        gh_send[i] = part.astype(BF16)

        @pl.when(i == x)
        def _():
            gh_own[...] = part

        return carry

    lax.fori_loop(0, 4, hidden, 0)
    gh_c = [
        send(gh_send.at[mod4(x + d)], gh_recv.at[d - 1], dev(dx=d)) for d in (1, 3, 2)
    ]

    arrive(*gw_c)
    for i in range(16):
        rows = slice(i * 8, (i + 1) * 8)
        part = gw_own[rows]
        for k in range(3):
            wide = gw_recv[k, (i // 2) * 16 : (i // 2) * 16 + 16].astype(F32)
            part = part + wide[(i % 2) * 8 : (i % 2) * 8 + 8]
        w2_send[i] = jnp.concatenate([part[:, :256], part[:, 256:]], axis=0).astype(BF16)
    me = zh * 4 + x
    w2_recv[me] = w2_send[me]
    w2_c = [
        send(w2_send.at[mod4(zh + a) * 4 + mod4(x + b)], w2_recv.at[me], dev(dzh=a, dx=b))
        for a in (2, 1, 3, 0)
        for b in range(4)
        if a + b > 0
    ]

    arrive(*gh_c)
    gh_out[...] = gh_own[...] + sum(gh_recv[k].astype(F32) for k in range(3))
    arrive(*kls)
    k0 = lax.div(x, 2) * 4 + lax.rem(x, 2) * 2
    kl_out[...] = kl_buf[k0, 0:1] + kl_buf[k0 + 1, 0:1]

    arrive(*w2_c)
    for q in range(4):
        both = sum(w2_recv[a * 4 + q].astype(F32) for a in range(4))
        gw_out[:, q * 512 : q * 512 + 256] = both[:8]
        gw_out[:, q * 512 + 256 : (q + 1) * 512] = both[8:]
    for copy in started:
        copy.wait_send()


def body(teacher_hidden, teacher_head, student_hidden, student_head, teacher_rest, student_rest):
    vmem = pl.BlockSpec(memory_space=pltpu.VMEM)
    anywhere = pl.BlockSpec(memory_space=pl.ANY)
    kl, grad_head, grad_hidden = pl.pallas_call(
        distill_kernel,
        out_shape=(
            jax.ShapeDtypeStruct((1, 128), F32),
            jax.ShapeDtypeStruct((8, 2048), F32),
            jax.ShapeDtypeStruct((128, 512), F32),
        ),
        in_specs=[anywhere, anywhere, anywhere, vmem, vmem, vmem],
        out_specs=(vmem, vmem, vmem),
        scratch_shapes=[
            pltpu.VMEM((4, 16, 256), BF16),
            pltpu.VMEM((8, 128), F32),
            pltpu.VMEM((4, 128, 2048), BF16),
            pltpu.VMEM((4, 128, 512), BF16),
            pltpu.VMEM((16, 128, 512), BF16),
            pltpu.VMEM((16, 64, 256), BF16),
            pltpu.VMEM((512, 512), BF16),
            pltpu.VMEM((512, 512), BF16),
            pltpu.VMEM((4, 8, 128), F32),
            pltpu.VMEM((256, 512), F32),
            pltpu.VMEM((256, 512), F32),
            pltpu.VMEM((256, 512), F32),
            pltpu.VMEM((256, 512), F32),
            pltpu.VMEM((256, 512), F32),
            pltpu.VMEM((256, 512), F32),
            pltpu.VMEM((3, 64, 512), F32),
            pltpu.VMEM((3, 64, 512), F32),
            pltpu.VMEM((4, 64, 128), F32),
            pltpu.VMEM((8, 64, 512), BF16),
            pltpu.VMEM((8, 8, 128), F32),
            pltpu.VMEM((128, 512), F32),
            pltpu.VMEM((4, 128, 512), BF16),
            pltpu.VMEM((3, 128, 512), BF16),
            pltpu.VMEM((128, 512), F32),
            pltpu.VMEM((4, 128, 512), BF16),
            pltpu.VMEM((3, 128, 512), BF16),
            pltpu.VMEM((16, 16, 256), BF16),
            pltpu.VMEM((16, 16, 256), BF16),
            pltpu.SemaphoreType.DMA((N_COPY,)),
            pltpu.SemaphoreType.DMA((N_COPY,)),
            pltpu.SemaphoreType.DMA((3,)),
        ],
        compiler_params=pltpu.CompilerParams(
            collective_id=0, has_side_effects=True, vmem_limit_bytes=40 * 1024 * 1024
        ),
    )(
        teacher_hidden,
        teacher_head,
        student_hidden,
        student_head,
        teacher_rest.reshape(1, 128),
        student_rest.reshape(1, 128),
    )
    return kl.reshape(128), grad_head, grad_hidden


def solution(mesh):
    return jax.shard_map(
        body,
        mesh=mesh,
        in_specs=(
            P("fsdp", "role"),
            P(("role", "fsdp"), None),
            P("fsdp", "role"),
            P(("role", "fsdp"), None),
            P("fsdp"),
            P("fsdp"),
        ),
        out_specs=(P("fsdp"), P(("role", "fsdp"), None), P("fsdp", "role")),
        check_vma=False,
    )
```

time: 893 us -> 119 us (0.13)
  the two profiles are of different devices: /device:TPU:0 before, /device:TPU:1 now
where the time goes in v1:
time: 119 us
  Pallas kernels  112 us (94%)
  local copies, waits for them, and re-layouts  6.11 us (5%)
    pallas_call x1, Pallas kernels, body(): pl.pallas_call(distill_kernel, out_shape=(jax.ShapeDtypeStruct((1, 128),...  112 us
    unnamed x15, local copies, waits for them, and re-layouts  6.11 us

profile of v1, /device:TPU:1, one launch (start us, length us, event | category | flops | bytes accessed | tf_op | source)
XLA Modules:
  0.0 119.1 jit_solution(3373202186870312656)
XLA Ops:
  0.6 0.0 copy-start.4
  0.6 0.0 copy-start.5
  0.7 0.6 copy-done.4
  1.3 0.0 copy-done.5
  1.3 0.0 copy-start
  1.3 1.0 copy-done
  2.3 0.0 copy-start.1
  2.3 0.9 copy-done.1
  3.3 0.0 copy-start.2
  3.3 0.9 copy-done.2
  4.2 0.0 copy-start.3
  4.2 0.8 copy-done.3
  4.9 112.3 %shard_map.85 = (f32[1,128]{1,0:T(1,128)S(1)}, f32[8,2048]{1,0:T(8,128)S(1)}, f32[128,512]{1,0:T(8,128)S(1)}) custom-call(bf16[128,2048]{1,0:T(8,128)(2,1)S(1)} %copy-done, bf16[32,2048]{1,0:T(8,128)(2,1)S(1)} %copy-done.1, bf16[128,512]{1,0:T(8,128)(2,1)S(1)} %copy-done.2, bf16[8,2048]{1,0:T(8,128)(2,1)S(1)} %copy-done.3, f32[1,128]{1,0:T(1,128)S(1)} %bitcast.3, ...), custom_call_target="tpu_custom_call" | custom-call | tf_op jit(solution)/shard_map/pallas_call | solution.py:413
  117.2 0.5 copy.12
  117.7 0.6 copy.13
  118.4 0.7 copy.14
Async XLA Ops:
  0.6 0.7 copy-start.4
  0.6 0.7 copy-start.5
  1.3 1.0 copy-start
  2.3 0.9 copy-start.1
  3.3 0.9 copy-start.2
  4.2 0.8 copy-start.3

commit v2 on v1

--- a/solution.py
+++ b/solution.py
@@ -8,7 +8,7 @@
 MESH = pl.DeviceIdType.MESH
 F32 = jnp.float32
 BF16 = jnp.bfloat16
-N_COPY = 112
+N_COPY = 144
 
 
 def mod4(v):
@@ -19,12 +19,15 @@
     at_hbm,
     bt_hbm,
     as_hbm,
+    sh_hbm,
+    tr_hbm,
+    sr_hbm,
+    kl_out,
+    gw_out,
+    gh_out,
     sh_ref,
     tr_ref,
     sr_ref,
-    kl_out,
-    gw_out,
-    gh_out,
     bs_src,
     rest_src,
     at_buf,
@@ -104,9 +107,19 @@
         bt_buf.at[piece, pl.ds(row32, 32)],
         local_sem.at[2],
     )
+    small = [
+        pltpu.make_async_copy(src, dst, local_sem.at[3 + i])
+        for i, (src, dst) in enumerate(
+            ((sh_hbm, sh_ref), (tr_hbm, tr_ref), (sr_hbm, sr_ref))
+        )
+    ]
+    for copy in small:
+        copy.start()
+    own_bt.start()
     own_as.start()
-    own_bt.start()
     own_at.start()
+    for copy in small:
+        copy.wait()
 
     for q in range(4):
         wide = sh_ref[:, q * 512 : (q + 1) * 512].astype(F32)
@@ -132,68 +145,102 @@
                 dev(dx=d),
             )
         )
-    as_1 = [send(as_hbm, as_buf.at[x], dev(dx=d)) for d in (1, 3)]
     rests = [send(rest_src, rest_buf.at[x], dev(dx=d)) for d in (1, 3, 2)]
-    at_1 = [send(at_hbm, at_buf.at[x], dev(dx=d)) for d in (1, 3)]
-
-    def halves(buf, i, rows):
-        return buf.at[i, pl.ds(0, rows)], buf.at[i, pl.ds(rows, rows)]
-
-    def forward_x(first, buf):
-        arrive(first[0])
-        lo = halves(buf, mod4(x - 1), 64)[0]
-        a = send(lo, lo, dev(dx=1))
-        arrive(first[1])
-        hi = halves(buf, mod4(x + 1), 64)[1]
-        b = send(hi, hi, dev(dx=3))
-        return [a, b]
-
-    def both_y(buf, i):
-        return [send(buf.at[i], buf.at[i], dev(dy=d)) for d in (1, 3)]
-
-    def both_z(buf):
-        return [send(buf.at[piece], buf.at[piece], dev(dzh=d)) for d in (1, 3)]
-
-    def forward_z(first, buf, rows):
-        arrive(first[0])
-        i = mod4(zh - 1) * 4 + y
-        lo = halves(buf, i, rows)[0]
-        a = send(lo, lo, dev(dzh=1))
-        ya = both_y(buf, i)
-        arrive(first[1])
-        i = mod4(zh + 1) * 4 + y
-        hi = halves(buf, i, rows)[1]
-        b = send(hi, hi, dev(dzh=3))
-        yb = both_y(buf, i)
-        return [a, b], ya, yb
-
-    def forward_y(first, buf, zi, rows):
-        arrive(first[0])
-        lo = halves(buf, zi * 4 + mod4(y - 1), rows)[0]
-        a = send(lo, lo, dev(dy=1))
-        arrive(first[1])
-        hi = halves(buf, zi * 4 + mod4(y + 1), rows)[1]
-        b = send(hi, hi, dev(dy=3))
-        return [a, b]
+
+    order = ((1, 0), (3, 1), (1, 1), (3, 0))
+
+    def unit(buf, i, h, rows):
+        return buf.at[i, pl.ds(h * rows, rows)]
+
+    def pass_on(buf, i, h, rows, to):
+        ref = unit(buf, i, h, rows)
+        return send(ref, ref, to)
+
+    def x_start(src, buf):
+        return {
+            (d, h): send(src.at[pl.ds(h * 64, 64)], unit(buf, x, h, 64), dev(dx=d))
+            for d, h in order
+        }
+
+    def x_forward(sent, buf):
+        arrive(sent[1, 0])
+        a = pass_on(buf, mod4(x - 1), 0, 64, dev(dx=1))
+        arrive(sent[3, 1])
+        b = pass_on(buf, mod4(x + 1), 1, 64, dev(dx=3))
+        return [sent[1, 1], sent[3, 0], a, b]
+
+    class Head:
+        def __init__(self, buf, rows):
+            self.buf, self.rows = buf, rows
+            self.zs, self.ys, self.last = {}, {}, []
+
+        def z_start(self, which):
+            for d, h in which:
+                self.zs[d, h] = pass_on(self.buf, piece, h, self.rows, dev(dzh=d))
+
+        def z_forward(self):
+            arrive(self.zs[1, 0])
+            a = pass_on(self.buf, prev * 4 + y, 0, self.rows, dev(dzh=1))
+            arrive(self.zs[3, 1])
+            b = pass_on(self.buf, nxt * 4 + y, 1, self.rows, dev(dzh=3))
+            self.zf = (a, b)
+
+        def y_start(self, name, zi, h):
+            for d in (1, 3):
+                self.ys[name, h, d] = pass_on(
+                    self.buf, zi * 4 + y, h, self.rows, dev(dy=d)
+                )
+
+        def y_forward(self, name, zi, h):
+            d = 1 if h == 0 else 3
+            arrive(self.ys[name, h, d])
+            i = zi * 4 + mod4(y - 1 if h == 0 else y + 1)
+            self.last.append(pass_on(self.buf, i, h, self.rows, dev(dy=d)))
+            self.last.append(self.ys[name, h, 4 - d])
 
     prev, nxt, far = mod4(zh - 1), mod4(zh + 1), mod4(zh + 2)
+    st, te = Head(bs_buf, 32), Head(bt_buf, 64)
+
+    as_1 = x_start(as_hbm, as_buf)
+    at_1 = x_start(at_hbm, at_buf)
 
     arrive(*bs_a2a)
-    bs_z = both_z(bs_buf)
-    bs_y0 = both_y(bs_buf, piece)
+    st.z_start(order)
+    st.y_start("own", zh, 0)
+    st.y_start("own", zh, 1)
     own_bt.wait()
     arrive(*bt_a2a)
-    bt_z = both_z(bt_buf)
-    bt_y0 = both_y(bt_buf, piece)
-
-    as_2 = forward_x(as_1, as_buf)
-    bs_z2, bs_y1, bs_y2 = forward_z(bs_z, bs_buf, 32)
-    bs_f0 = forward_y(bs_y0, bs_buf, zh, 32)
-    bt_f0 = forward_y(bt_y0, bt_buf, zh, 64)
-    bs_f1 = forward_y(bs_y1, bs_buf, prev, 32)
-    bs_f2 = forward_y(bs_y2, bs_buf, nxt, 32)
-    arrive(*bs_z2)
-    bs_y3 = both_y(bs_buf, far * 4 + y)
+    te.z_start(order[:2])
+    te.y_start("own", zh, 0)
+    te.y_start("own", zh, 1)
+
+    st.z_forward()
+    te.z_start(order[2:])
+    st.y_start("prev", prev, 0)
+    st.y_start("next", nxt, 1)
+    st.y_forward("own", zh, 0)
+    st.y_forward("own", zh, 1)
+    as_2 = x_forward(as_1, as_buf)
+    arrive(st.zs[1, 1])
+    st.y_start("prev", prev, 1)
+    arrive(st.zs[3, 0])
+    st.y_start("next", nxt, 0)
+    st.y_forward("prev", prev, 0)
+    st.y_forward("next", nxt, 1)
+    te.y_forward("own", zh, 0)
+    te.y_forward("own", zh, 1)
+    arrive(st.zf[0])
+    st.y_start("far", far, 0)
+    arrive(st.zf[1])
+    st.y_start("far", far, 1)
+    st.y_forward("prev", prev, 1)
+    st.y_forward("next", nxt, 0)
+
+    te.z_forward()
+    te.y_start("prev", prev, 0)
+    te.y_start("next", nxt, 1)
+    st.y_forward("far", far, 0)
+    st.y_forward("far", far, 1)
 
     own_as.wait()
     arrive(*as_2)
@@ -209,17 +256,15 @@
 
     lax.fori_loop(0, 4, turn, 0)
 
-    bs_f3 = forward_y(bs_y3, bs_buf, far, 32)
-    arrive(*bs_f0, *bs_f1, *bs_f2, *bs_f3)
+    arrive(*st.last)
     for i in range(16):
         tall = bs_buf[i].astype(F32).reshape(4, 2, 8, 256)
         rows = slice(i * 32, (i + 1) * 32)
         bs_full[rows, :256] = tall[:, 0].reshape(32, 256).astype(BF16)
         bs_full[rows, 256:] = tall[:, 1].reshape(32, 256).astype(BF16)
 
-    def logits(a_buf, b_of, out, half):
-        a = a_buf[pl.ds(half * 2, 2)]
-        a = a.reshape(256, a.shape[-1])
+    def logits(a_buf, b_of, out, slot):
+        a = a_buf[slot]
 
         def column(i, carry):
             cols = pl.ds(pl.multiple_of(i * 256, 256), 256)
@@ -228,47 +273,61 @@
 
         lax.fori_loop(0, 2, column, 0)
 
+    def both_cores(a_buf, b_of, out_send, out_recv, out_own):
+        swaps = []
+        for k in range(2):
+            logits(a_buf, b_of, out_send.at[k], (1 - c) * 2 + k)
+            swaps.append(send(out_send.at[k], out_recv.at[k], dev(dc=1)))
+        for k in range(2):
+            logits(a_buf, b_of, out_own.at[k], c * 2 + k)
+        return swaps
+
     def student_b(cols):
         return bs_full[:, cols]
 
-    logits(as_buf, student_b, cs_send, 1 - c)
-    cs_swap = send(cs_send, cs_recv, dev(dc=1))
-    logits(as_buf, student_b, cs_own, c)
-
-    at_2 = forward_x(at_1, at_buf)
-    bt_z2, bt_y1, bt_y2 = forward_z(bt_z, bt_buf, 64)
-    bt_f1 = forward_y(bt_y1, bt_buf, prev, 64)
-    bt_f2 = forward_y(bt_y2, bt_buf, nxt, 64)
-    arrive(*bt_z2)
-    bt_y3 = both_y(bt_buf, far * 4 + y)
-
-    def scatter_z(swap, own, recv, zrecv):
-        arrive(swap)
-        own[...] = own[...] + recv[...]
+    cs_swap = both_cores(as_buf, student_b, cs_send, cs_recv, cs_own)
+
+    def tokens_of(ref, chip):
+        return ref.at[lax.div(chip, 2), pl.ds(pl.multiple_of(lax.rem(chip, 2) * 64, 64), 64)]
+
+    def scatter_z(swaps, own, recv, zrecv):
+        arrive(*swaps)
         copies = []
-        for d in (1, 3, 2):
-            rows = pl.ds(pl.multiple_of(mod4(zl + d) * 64, 64), 64)
-            copies.append(send(own.at[rows], zrecv.at[d - 1], dev(dzl=d)))
+        for d in (2, 1, 3, 0):
+            mine, theirs = tokens_of(own, mod4(zl + d)), tokens_of(recv, mod4(zl + d))
+            mine[...] = mine[...] + theirs[...]
+            if d > 0:
+                copies.append(send(mine, zrecv.at[d - 1], dev(dzl=d)))
         return copies
 
+    te.y_forward("prev", prev, 0)
+    te.y_forward("next", nxt, 1)
+    at_2 = x_forward(at_1, at_buf)
+    arrive(te.zs[1, 1])
+    te.y_start("prev", prev, 1)
+    arrive(te.zs[3, 0])
+    te.y_start("next", nxt, 0)
+    arrive(te.zf[0])
+    te.y_start("far", far, 0)
+    arrive(te.zf[1])
+    te.y_start("far", far, 1)
     cs_z = scatter_z(cs_swap, cs_own, cs_recv, zs_recv)
-    bt_f3 = forward_y(bt_y3, bt_buf, far, 64)
-    arrive(*bt_f0, *bt_f1, *bt_f2, *bt_f3)
+    te.y_forward("prev", prev, 1)
+    te.y_forward("next", nxt, 0)
+    te.y_forward("far", far, 0)
+    te.y_forward("far", far, 1)
+    arrive(*te.last)
     own_at.wait()
     arrive(*at_2)
 
     def teacher_b(cols):
         return bt_buf[:, :, cols].reshape(2048, 256)
 
-    logits(at_buf, teacher_b, ct_send, 1 - c)
-    ct_swap = send(ct_send, ct_recv, dev(dc=1))
-    logits(at_buf, teacher_b, ct_own, c)
+    ct_swap = both_cores(at_buf, teacher_b, ct_send, ct_recv, ct_own)
     ct_z = scatter_z(ct_swap, ct_own, ct_recv, zt_recv)
 
-    mine = pl.ds(pl.multiple_of(zl * 64, 64), 64)
-
     def scaled(own, zrecv):
-        return (own[mine] + zrecv[0] + zrecv[1] + zrecv[2]) * 0.5
+        return (tokens_of(own, zl)[...] + zrecv[0] + zrecv[1] + zrecv[2]) * 0.5
 
     arrive(*cs_z)
     s = scaled(cs_own, zs_recv)
@@ -409,7 +468,7 @@
 
 def body(teacher_hidden, teacher_head, student_hidden, student_head, teacher_rest, student_rest):
     vmem = pl.BlockSpec(memory_space=pltpu.VMEM)
-    anywhere = pl.BlockSpec(memory_space=pl.ANY)
+    hbm = pl.BlockSpec(memory_space=pltpu.HBM)
     kl, grad_head, grad_hidden = pl.pallas_call(
         distill_kernel,
         out_shape=(
@@ -417,9 +476,12 @@
             jax.ShapeDtypeStruct((8, 2048), F32),
             jax.ShapeDtypeStruct((128, 512), F32),
         ),
-        in_specs=[anywhere, anywhere, anywhere, vmem, vmem, vmem],
+        in_specs=[hbm] * 6,
         out_specs=(vmem, vmem, vmem),
         scratch_shapes=[
+            pltpu.VMEM((8, 2048), BF16),
+            pltpu.VMEM((1, 128), F32),
+            pltpu.VMEM((1, 128), F32),
             pltpu.VMEM((4, 16, 256), BF16),
             pltpu.VMEM((8, 128), F32),
             pltpu.VMEM((4, 128, 2048), BF16),
@@ -429,12 +491,12 @@
             pltpu.VMEM((512, 512), BF16),
             pltpu.VMEM((512, 512), BF16),
             pltpu.VMEM((4, 8, 128), F32),
-            pltpu.VMEM((256, 512), F32),
-            pltpu.VMEM((256, 512), F32),
-            pltpu.VMEM((256, 512), F32),
-            pltpu.VMEM((256, 512), F32),
-            pltpu.VMEM((256, 512), F32),
-            pltpu.VMEM((256, 512), F32),
+            pltpu.VMEM((2, 128, 512), F32),
+            pltpu.VMEM((2, 128, 512), F32),
+            pltpu.VMEM((2, 128, 512), F32),
+            pltpu.VMEM((2, 128, 512), F32),
+            pltpu.VMEM((2, 128, 512), F32),
+            pltpu.VMEM((2, 128, 512), F32),
             pltpu.VMEM((3, 64, 512), F32),
             pltpu.VMEM((3, 64, 512), F32),
             pltpu.VMEM((4, 64, 128), F32),
@@ -450,10 +512,10 @@
             pltpu.VMEM((16, 16, 256), BF16),
             pltpu.SemaphoreType.DMA((N_COPY,)),
             pltpu.SemaphoreType.DMA((N_COPY,)),
-            pltpu.SemaphoreType.DMA((3,)),
+            pltpu.SemaphoreType.DMA((6,)),
         ],
         compiler_params=pltpu.CompilerParams(
-            collective_id=0, has_side_effects=True, vmem_limit_bytes=40 * 1024 * 1024
+            collective_id=0, has_side_effects=True, vmem_limit_bytes=63 * 1024 * 1024
         ),
     )(
         teacher_hidden,

time: 119 us -> 114 us (0.958)
  Pallas kernels: 112 us -> 109 us
  local copies, waits for them, and re-layouts: 6.11 us -> 4.26 us
    pallas_call x1, Pallas kernels: 112 us -> 109 us  [body(): pl.pallas_call(distill_kernel, out_shape=(jax.ShapeDtypeStruct((1, 128),...]
    unnamed x15 -> x5, local copies, waits for them, and re-layouts: 6.11 us -> 4.26 us
where the time goes in v2:
time: 114 us
  Pallas kernels  109 us (96%)
  local copies, waits for them, and re-layouts  4.26 us (4%)
    pallas_call x1, Pallas kernels, body(): pl.pallas_call(distill_kernel, out_shape=(jax.ShapeDtypeStruct((1, 128),...  109 us
    unnamed x5, local copies, waits for them, and re-layouts  4.26 us

profile of v2, /device:TPU:1, one launch (start us, length us, event | category | flops | bytes accessed | tf_op | source)
XLA Modules:
  0.0 113.7 jit_solution(6894989326721253308)
XLA Ops:
  0.6 108.8 %shard_map.85 = (f32[1,128]{1,0:T(1,128)}, f32[8,2048]{1,0:T(8,128)}, f32[128,512]{1,0:T(8,128)}) custom-call(bf16[128,2048]{1,0:T(8,128)(2,1)} %at_hbm.1, bf16[32,2048]{1,0:T(8,128)(2,1)} %bt_hbm.1, bf16[128,512]{1,0:T(8,128)(2,1)} %as_hbm.1, bf16[8,2048]{1,0:T(8,128)(2,1)} %sh_hbm.1, f32[1,128]{1,0:T(1,128)} %bitcast.3, f32[1,128]{1,0:T(1,128)} %bitcast.4), custom_call_target="tpu_custom_call" | custom-call | tf_op jit(solution)/shard_map/pallas_call | solution.py:472
  109.4 0.0 copy-start
  109.4 0.6 copy-done
  110.0 0.5 copy.12
  110.6 1.5 %copy.13 = f32[8,2048]{1,0:T(8,128)} copy(f32[8,2048]{1,0:T(8,128)} %get-tuple-element.13) | data formatting | bytes 131072
  112.0 1.7 %copy.14 = f32[128,512]{1,0:T(8,128)} copy(f32[128,512]{1,0:T(8,128)} %get-tuple-element.14) | data formatting | bytes 524288
Async XLA Ops:
  109.4 0.6 copy-start

commit v3 on v2

--- a/solution.py
+++ b/solution.py
@@ -54,8 +54,13 @@
     gw_own,
     gw_send,
     gw_recv,
-    w2_send,
-    w2_recv,
+    w_own,
+    w_send,
+    w_recv,
+    x_send,
+    kl_vmem,
+    gw_vmem,
+    gh_vmem,
     send_sem,
     recv_sem,
     local_sem,
@@ -90,7 +95,7 @@
         for copy in copies:
             copy.wait_recv()
 
-    partners = [dev(dzh=a, dx=b) for a in range(4) for b in range(4) if a + b > 0]
+    partners = [dev(dzh=d) for d in (1, 2, 3)] + [dev(dx=d) for d in (1, 2, 3)]
     partners += [dev(dy=d) for d in (1, 2, 3)]
     partners += [dev(dzl=a, dc=b) for a in range(4) for b in range(2) if a + b > 0]
     barrier = pltpu.get_barrier_semaphore()
@@ -344,26 +349,21 @@
     stat = jnp.zeros((64, 128), F32)
     for i, col in enumerate((mt, et, ms, es, ws)):
         stat = jnp.where(lane == i, col, stat)
-    stat_buf[x] = stat
+    flat = stat.T[:8]
+    stat_buf[x] = jnp.concatenate([flat, flat], axis=1)
     stats = [send(stat_buf.at[x], stat_buf.at[x], dev(dx=d)) for d in (1, 3, 2)]
-
     arrive(*rests)
-    rests8 = rest_buf[c * 2 + lax.div(zl, 2)]
-    token = lax.broadcasted_iota(jnp.int32, (64, 128), 0) + lax.rem(zl, 2) * 64
-    hit = token == lane
-    rest_t = jnp.sum(jnp.where(hit, rests8[0:1], 0.0), axis=-1, keepdims=True)
-    rest_s = jnp.sum(jnp.where(hit, rests8[1:2], 0.0), axis=-1, keepdims=True)
-
     arrive(*stats)
     got = [stat_buf[i] for i in range(4)]
+    rests8 = rest_buf[c * 2 + lax.div(zl, 2)]
 
     def log_add(a, b):
         top = jnp.maximum(a, b)
         return top + jnp.log(jnp.exp(a - top) + jnp.exp(b - top))
 
     def whole(k):
-        tops = [v[:, k : k + 1] for v in got]
-        sums = [v[:, k + 1 : k + 2] for v in got]
+        tops = [v[k : k + 1] for v in got]
+        sums = [v[k + 1 : k + 2] for v in got]
         top = jnp.maximum(jnp.maximum(tops[0], tops[1]), jnp.maximum(tops[2], tops[3]))
         scale = [jnp.exp(m - top) for m in tops]
         total = sum(a * b for a, b in zip(sums, scale))
@@ -371,19 +371,29 @@
 
     top_t, scale_t, sum_t = whole(0)
     top_s, _, sum_s = whole(2)
-    norm_t = log_add(top_t + jnp.log(sum_t), rest_t)
-    norm_s = log_add(top_s + jnp.log(sum_s), rest_s)
-    grad = (8.0 * (jnp.exp(s - norm_s) - jnp.exp(t - norm_t))).astype(BF16)
+    norm_t = log_add(top_t + jnp.log(sum_t), rests8[0:1])
+    norm_s = log_add(top_s + jnp.log(sum_s), rests8[1:2])
+    upper = lax.rem(zl, 2)
+    square = lax.broadcasted_iota(jnp.int32, (128, 128), 0)
+    turned = jnp.where(square == 0, norm_t, norm_s).T
+    turned = jnp.where(upper == 0, turned[:64], turned[64:])
+    col_t, col_s = turned[:, 0:1], turned[:, 1:2]
+
     j = c * 4 + zl
-    g_buf[j] = grad
-    g_chip = send(g_buf.at[j], g_buf.at[j], dev(dc=1))
-    g_z = [send(g_buf.at[j], g_buf.at[j], dev(dzl=d)) for d in (1, 3, 2)]
-
-    weighted = sum(v[:, 4:5] * b for v, b in zip(got, scale_t))
+    g_z, g_chip = [], []
+    for v in range(2):
+        cols = slice(v * 256, (v + 1) * 256)
+        gap = jnp.exp(s[:, cols] - col_s) - jnp.exp(t[:, cols] - col_t)
+        g_buf[v, j] = (8.0 * gap).astype(BF16)
+        mine = g_buf.at[v, j]
+        g_z.append([send(mine, mine, dev(dzl=d)) for d in (2, 1, 3)])
+        g_chip.append(send(mine, mine, dev(dc=1)))
+
+    weighted = sum(v[4:5] * b for v, b in zip(got, scale_t))
     inside = jnp.exp(top_t - norm_t)
     kl = 16.0 * (weighted * inside - sum_t * inside * (norm_t - norm_s))
-    kl_row = jnp.sum(jnp.where(hit, kl, 0.0), axis=0, keepdims=True)
-    kl_buf[j] = jnp.broadcast_to(kl_row, (8, 128))
+    half_of = lax.div(lax.broadcasted_iota(jnp.int32, (1, 128), 1), 64)
+    kl_buf[j] = jnp.broadcast_to(jnp.where(half_of == upper, kl, 0.0), (8, 128))
     kls = [
         send(kl_buf.at[j], kl_buf.at[j], dev(dzl=a, dc=b))
         for a in range(4)
@@ -391,93 +401,114 @@
         if a + b > 0
     ]
 
-    g_f = []
-    for copy, d in zip(g_z, (1, 3, 2)):
-        arrive(copy)
-        k = c * 4 + mod4(zl - d)
-        g_f.append(send(g_buf.at[k], g_buf.at[k], dev(dc=1)))
-    arrive(g_chip, *g_f)
-
-    g = g_buf[...].reshape(512, 512)
-
-    def head(i, carry):
-        rows = pl.ds(pl.multiple_of(i * 128, 128), 128)
-        part = jnp.dot(as_t[rows], g, preferred_element_type=F32)
-        gw_send[i] = part.astype(BF16)
-
-        @pl.when(i == y)
-        def _():
-            gw_own[...] = part
-
-        return carry
-
-    lax.fori_loop(0, 4, head, 0)
-    gw_c = [
-        send(gw_send.at[mod4(y + d)], gw_recv.at[d - 1], dev(dy=d)) for d in (1, 3, 2)
-    ]
-
-    def hidden(i, carry):
-        rows = g_buf[pl.ds(i * 2, 2)].reshape(128, 512)
-        part = lax.dot_general(
-            rows, bs_full[...], (((1,), (1,)), ((), ())), preferred_element_type=F32
+    gw_c, gh_c = [], []
+    for v in range(2):
+        g_f = []
+        for copy, d in zip(g_z[v], (2, 1, 3)):
+            arrive(copy)
+            theirs = g_buf.at[v, c * 4 + mod4(zl - d)]
+            g_f.append(send(theirs, theirs, dev(dc=1)))
+        arrive(g_chip[v], *g_f)
+
+        g = g_buf[v].reshape(512, 256)
+        sent = []
+        for d in (2, 1, 3, 0):
+            rows = pl.ds(pl.multiple_of(mod4(y + d) * 128, 128), 128)
+            part = jnp.dot(as_t[rows], g, preferred_element_type=F32)
+            if d == 0:
+                gw_own[v] = part
+            else:
+                gw_send[v, d - 1] = part.astype(BF16)
+                sent.append(send(gw_send.at[v, d - 1], gw_recv.at[v, d - 1], dev(dy=d)))
+        gw_c.append(sent)
+
+        for d in (2, 1, 3, 0):
+            rows = g_buf[v, pl.ds(mod4(x + d) * 2, 2)].reshape(128, 256)
+            part = lax.dot_general(
+                rows,
+                bs_full[:, v * 256 : (v + 1) * 256],
+                (((1,), (1,)), ((), ())),
+                preferred_element_type=F32,
+            )
+            if v == 0:
+                gh_own[d] = part
+            elif d == 0:
+                gh_own[0] = gh_own[0] + part
+            else:
+                gh_send[d - 1] = (gh_own[d] + part).astype(BF16)
+                gh_c.append(send(gh_send.at[d - 1], gh_recv.at[d - 1], dev(dx=d)))
+
+    w_c = []
+    for v in range(2):
+        arrive(*gw_c[v])
+        total = gw_own[v] + sum(gw_recv[v, k].astype(F32) for k in range(3))
+        total = total.reshape(4, 32, 256)
+        w_own[v] = total
+        w_send[v] = total.astype(BF16)
+        w_c.append(
+            [
+                send(w_send.at[v, mod4(zh + d)], w_recv.at[v, d - 1], dev(dzh=d))
+                for d in (2, 1, 3)
+            ]
         )
-        gh_send[i] = part.astype(BF16)
-
-        @pl.when(i == x)
-        def _():
-            gh_own[...] = part
-
-        return carry
-
-    lax.fori_loop(0, 4, hidden, 0)
-    gh_c = [
-        send(gh_send.at[mod4(x + d)], gh_recv.at[d - 1], dev(dx=d)) for d in (1, 3, 2)
-    ]
-
-    arrive(*gw_c)
-    for i in range(16):
-        rows = slice(i * 8, (i + 1) * 8)
-        part = gw_own[rows]
-        for k in range(3):
-            wide = gw_recv[k, (i // 2) * 16 : (i // 2) * 16 + 16].astype(F32)
-            part = part + wide[(i % 2) * 8 : (i % 2) * 8 + 8]
-        w2_send[i] = jnp.concatenate([part[:, :256], part[:, 256:]], axis=0).astype(BF16)
-    me = zh * 4 + x
-    w2_recv[me] = w2_send[me]
-    w2_c = [
-        send(w2_send.at[mod4(zh + a) * 4 + mod4(x + b)], w2_recv.at[me], dev(dzh=a, dx=b))
-        for a in (2, 1, 3, 0)
-        for b in range(4)
-        if a + b > 0
-    ]
+
+    def write_out(src, dst, k):
+        copy = pltpu.make_async_copy(src, dst, local_sem.at[k])
+        copy.start()
+        return copy
 
     arrive(*gh_c)
-    gh_out[...] = gh_own[...] + sum(gh_recv[k].astype(F32) for k in range(3))
+    gh_vmem[...] = gh_own[0] + sum(gh_recv[k].astype(F32) for k in range(3))
+    outs = [write_out(gh_vmem, gh_out, 6)]
     arrive(*kls)
     k0 = lax.div(x, 2) * 4 + lax.rem(x, 2) * 2
-    kl_out[...] = kl_buf[k0, 0:1] + kl_buf[k0 + 1, 0:1]
-
-    arrive(*w2_c)
-    for q in range(4):
-        both = sum(w2_recv[a * 4 + q].astype(F32) for a in range(4))
-        gw_out[:, q * 512 : q * 512 + 256] = both[:8]
-        gw_out[:, q * 512 + 256 : (q + 1) * 512] = both[8:]
+    kl_vmem[...] = kl_buf[k0, 0:1] + kl_buf[k0 + 1, 0:1]
+    outs.append(write_out(kl_vmem, kl_out, 7))
+
+    x_c = []
+    for v in range(2):
+        arrive(*w_c[v])
+        rows = w_own[v, zh] + sum(w_recv[v, k].astype(F32) for k in range(3))
+        x_send[v] = rows.reshape(4, 8, 256)
+        cols = pl.ds(pl.multiple_of(x * 512 + v * 256, 256), 256)
+        gw_vmem[:, cols] = x_send[v, x]
+        x_c += [
+            send(x_send.at[v, mod4(x + d)], gw_vmem.at[:, cols], dev(dx=d))
+            for d in (2, 1, 3)
+        ]
     for copy in started:
         copy.wait_send()
+    arrive(*x_c)
+    outs.append(write_out(gw_vmem, gw_out, 8))
+    for copy in outs:
+        copy.wait()
+
+
+def settle_kernel(kl_in, gw_in, gh_in, kl_out, gw_out, gh_out, kl_vmem, gw_vmem, gh_vmem, sem):
+    ways = ((gh_in, gh_vmem, gh_out), (gw_in, gw_vmem, gw_out), (kl_in, kl_vmem, kl_out))
+    into = [pltpu.make_async_copy(a, b, sem.at[i]) for i, (a, b, _) in enumerate(ways)]
+    onto = [pltpu.make_async_copy(b, o, sem.at[3 + i]) for i, (_, b, o) in enumerate(ways)]
+    for copy in into:
+        copy.start()
+    for first, then in zip(into, onto):
+        first.wait()
+        then.start()
+    for copy in onto:
+        copy.wait()
 
 
 def body(teacher_hidden, teacher_head, student_hidden, student_head, teacher_rest, student_rest):
-    vmem = pl.BlockSpec(memory_space=pltpu.VMEM)
     hbm = pl.BlockSpec(memory_space=pltpu.HBM)
-    kl, grad_head, grad_hidden = pl.pallas_call(
+    out_shape = (
+        jax.ShapeDtypeStruct((1, 128), F32),
+        jax.ShapeDtypeStruct((8, 2048), F32),
+        jax.ShapeDtypeStruct((128, 512), F32),
+    )
+    results = pl.pallas_call(
         distill_kernel,
-        out_shape=(
-            jax.ShapeDtypeStruct((1, 128), F32),
-            jax.ShapeDtypeStruct((8, 2048), F32),
-            jax.ShapeDtypeStruct((128, 512), F32),
-        ),
+        out_shape=out_shape,
         in_specs=[hbm] * 6,
-        out_specs=(vmem, vmem, vmem),
+        out_specs=(hbm, hbm, hbm),
         scratch_shapes=[
             pltpu.VMEM((8, 2048), BF16),
             pltpu.VMEM((1, 128), F32),
@@ -499,20 +530,25 @@
             pltpu.VMEM((2, 128, 512), F32),
             pltpu.VMEM((3, 64, 512), F32),
             pltpu.VMEM((3, 64, 512), F32),
-            pltpu.VMEM((4, 64, 128), F32),
-            pltpu.VMEM((8, 64, 512), BF16),
+            pltpu.VMEM((4, 8, 128), F32),
+            pltpu.VMEM((2, 8, 64, 256), BF16),
             pltpu.VMEM((8, 8, 128), F32),
+            pltpu.VMEM((4, 128, 512), F32),
+            pltpu.VMEM((3, 128, 512), BF16),
+            pltpu.VMEM((3, 128, 512), BF16),
+            pltpu.VMEM((2, 128, 256), F32),
+            pltpu.VMEM((2, 3, 128, 256), BF16),
+            pltpu.VMEM((2, 3, 128, 256), BF16),
+            pltpu.VMEM((2, 4, 32, 256), F32),
+            pltpu.VMEM((2, 4, 32, 256), BF16),
+            pltpu.VMEM((2, 3, 32, 256), BF16),
+            pltpu.VMEM((2, 4, 8, 256), F32),
+            pltpu.VMEM((1, 128), F32),
+            pltpu.VMEM((8, 2048), F32),
             pltpu.VMEM((128, 512), F32),
-            pltpu.VMEM((4, 128, 512), BF16),
-            pltpu.VMEM((3, 128, 512), BF16),
-            pltpu.VMEM((128, 512), F32),
-            pltpu.VMEM((4, 128, 512), BF16),
-            pltpu.VMEM((3, 128, 512), BF16),
-            pltpu.VMEM((16, 16, 256), BF16),
-            pltpu.VMEM((16, 16, 256), BF16),
             pltpu.SemaphoreType.DMA((N_COPY,)),
             pltpu.SemaphoreType.DMA((N_COPY,)),
-            pltpu.SemaphoreType.DMA((6,)),
+            pltpu.SemaphoreType.DMA((9,)),
         ],
         compiler_params=pltpu.CompilerParams(
             collective_id=0, has_side_effects=True, vmem_limit_bytes=63 * 1024 * 1024
@@ -525,6 +561,19 @@
         teacher_rest.reshape(1, 128),
         student_rest.reshape(1, 128),
     )
+    kl, grad_head, grad_hidden = pl.pallas_call(
+        settle_kernel,
+        out_shape=out_shape,
+        in_specs=[hbm] * 3,
+        out_specs=(hbm, hbm, hbm),
+        scratch_shapes=[
+            pltpu.VMEM((1, 128), F32),
+            pltpu.VMEM((8, 2048), F32),
+            pltpu.VMEM((128, 512), F32),
+            pltpu.SemaphoreType.DMA((6,)),
+        ],
+        compiler_params=pltpu.CompilerParams(vmem_limit_bytes=63 * 1024 * 1024),
+    )(*results)
     return kl.reshape(128), grad_head, grad_hidden
 
 

time: 114 us -> 106 us (0.930)
  local copies, waits for them, and re-layouts: 4.26 us -> 0 us
  Pallas kernels: 109 us -> 105 us
    unnamed x5 -> x0, local copies, waits for them, and re-layouts: 4.26 us -> none
    pallas_call x1 -> x2, Pallas kernels: 109 us -> 105 us  [the longest x1 103 us: body(): pl.pallas_call(distill_kernel, out_shape=out_shape, in_specs=[hbm] * 6, o...]
where the time goes in v3:
time: 106 us
  Pallas kernels  105 us (99%)
    pallas_call x1, Pallas kernels, body(): pl.pallas_call(distill_kernel, out_shape=out_shape, in_specs=[hbm] * 6, o...  103 us

profile of v3, /device:TPU:1, one launch (start us, length us, event | category | flops | bytes accessed | tf_op | source)
XLA Modules:
  0.0 105.6 jit_solution(17225963425978993081)
XLA Ops:
  0.6 103.2 %shard_map.85 = (f32[1,128]{1,0:T(1,128)}, f32[8,2048]{1,0:T(8,128)}, f32[128,512]{1,0:T(8,128)}) custom-call(bf16[128,2048]{1,0:T(8,128)(2,1)} %at_hbm.1, bf16[32,2048]{1,0:T(8,128)(2,1)} %bt_hbm.1, bf16[128,512]{1,0:T(8,128)(2,1)} %as_hbm.1, bf16[8,2048]{1,0:T(8,128)(2,1)} %sh_hbm.1, f32[1,128]{1,0:T(1,128)} %bitcast.3, f32[1,128]{1,0:T(1,128)} %bitcast.4), custom_call_target="tpu_custom_call" | custom-call | tf_op jit(solution)/shard_map/pallas_call | solution.py:507
  103.9 1.7 %shard_map.86 = (f32[1,128]{1,0:T(1,128)}, f32[8,2048]{1,0:T(8,128)}, f32[128,512]{1,0:T(8,128)}) custom-call(f32[1,128]{1,0:T(1,128)} %get-tuple-element.9.kl_in, f32[8,2048]{1,0:T(8,128)} %get-tuple-element.10.gw_in, f32[128,512]{1,0:T(8,128)} %get-tuple-element.11.gh_in), custom_call_target="tpu_custom_call" | custom-call | tf_op jit(solution)/shard_map/pallas_call | solution.py:564

commit v4 on v3

--- a/solution.py
+++ b/solution.py
@@ -43,6 +43,8 @@
     cs_send,
     cs_recv,
     cs_own,
+    zt_send,
+    zs_send,
     zt_recv,
     zs_recv,
     stat_buf,
@@ -75,7 +77,7 @@
         f = (mod4(zh + dzh) * 4 + mod4(y + dy)) * 4 + mod4(x + dx)
         return (r, f)
 
-    started = []
+    started, pending = [], []
 
     def send(src, dst, to):
         k = len(started)
@@ -89,7 +91,12 @@
         )
         copy.start()
         started.append(copy)
+        pending.append(copy)
         return copy
+
+    def drain():
+        while pending:
+            pending.pop(0).wait_send()
 
     def arrive(*copies):
         for copy in copies:
@@ -223,9 +230,9 @@
     te.z_start(order[2:])
     st.y_start("prev", prev, 0)
     st.y_start("next", nxt, 1)
+    as_2 = x_forward(as_1, as_buf)
     st.y_forward("own", zh, 0)
     st.y_forward("own", zh, 1)
-    as_2 = x_forward(as_1, as_buf)
     arrive(st.zs[1, 1])
     st.y_start("prev", prev, 1)
     arrive(st.zs[3, 0])
@@ -234,18 +241,16 @@
     st.y_forward("next", nxt, 1)
     te.y_forward("own", zh, 0)
     te.y_forward("own", zh, 1)
+    st.y_forward("prev", prev, 1)
+    st.y_forward("next", nxt, 0)
+    at_2 = x_forward(at_1, at_buf)
+    te.z_forward()
+    te.y_start("prev", prev, 0)
+    te.y_start("next", nxt, 1)
     arrive(st.zf[0])
     st.y_start("far", far, 0)
     arrive(st.zf[1])
     st.y_start("far", far, 1)
-    st.y_forward("prev", prev, 1)
-    st.y_forward("next", nxt, 0)
-
-    te.z_forward()
-    te.y_start("prev", prev, 0)
-    te.y_start("next", nxt, 1)
-    st.y_forward("far", far, 0)
-    st.y_forward("far", far, 1)
 
     own_as.wait()
     arrive(*as_2)
@@ -261,6 +266,10 @@
 
     lax.fori_loop(0, 4, turn, 0)
 
+    st.y_forward("far", far, 0)
+    st.y_forward("far", far, 1)
+    te.y_forward("prev", prev, 0)
+    te.y_forward("next", nxt, 1)
     arrive(*st.last)
     for i in range(16):
         tall = bs_buf[i].astype(F32).reshape(4, 2, 8, 256)
@@ -268,71 +277,98 @@
         bs_full[rows, :256] = tall[:, 0].reshape(32, 256).astype(BF16)
         bs_full[rows, 256:] = tall[:, 1].reshape(32, 256).astype(BF16)
 
-    def logits(a_buf, b_of, out, slot):
-        a = a_buf[slot]
-
-        def column(i, carry):
-            cols = pl.ds(pl.multiple_of(i * 256, 256), 256)
-            out[:, cols] = jnp.dot(a, b_of(cols), preferred_element_type=F32)
-            return carry
-
-        lax.fori_loop(0, 2, column, 0)
-
-    def both_cores(a_buf, b_of, out_send, out_recv, out_own):
-        swaps = []
-        for k in range(2):
-            logits(a_buf, b_of, out_send.at[k], (1 - c) * 2 + k)
-            swaps.append(send(out_send.at[k], out_recv.at[k], dev(dc=1)))
-        for k in range(2):
-            logits(a_buf, b_of, out_own.at[k], c * 2 + k)
-        return swaps
-
-    def student_b(cols):
-        return bs_full[:, cols]
-
-    cs_swap = both_cores(as_buf, student_b, cs_send, cs_recv, cs_own)
+    def student_part(out, slot):
+        out[...] = jnp.dot(as_buf[slot], bs_full[...], preferred_element_type=F32)
+
+    cs_swap = []
+    for k in range(2):
+        student_part(cs_send.at[k], (1 - c) * 2 + k)
+        cs_swap.append(send(cs_send.at[k], cs_recv.at[k], dev(dc=1)))
+    for k in range(2):
+        student_part(cs_own.at[k], c * 2 + k)
 
     def tokens_of(ref, chip):
         return ref.at[lax.div(chip, 2), pl.ds(pl.multiple_of(lax.rem(chip, 2) * 64, 64), 64)]
 
-    def scatter_z(swaps, own, recv, zrecv):
+    def pack(v):
+        halves = []
+        for w in (v[:, :256], v[:, 256:]):
+            near = w.astype(BF16)
+            wide = near.astype(F32)
+            size = jnp.abs(wide)
+            fits = size > 1e-30
+            steps = (w - wide) * (1792.0 / jnp.where(fits, size, 1.0))
+            halves.append((near, jnp.round(jnp.where(fits, steps, 0.0))))
+        (n0, r0), (n1, r1) = halves
+        return n0, n1, (16.0 * r0 + r1).astype(BF16)
+
+    def unpack(ref):
+        both = ref[:, 512:].astype(F32)
+        r0 = jnp.round(both * 0.0625)
+        out = []
+        for i, r in enumerate((r0, both - 16.0 * r0)):
+            wide = ref[:, i * 256 : (i + 1) * 256].astype(F32)
+            out.append(wide + r * (jnp.abs(wide) * (1.0 / 1792.0)))
+        return jnp.concatenate(out, axis=1)
+
+    def scatter_z(swaps, own, recv, zsend, zrecv):
         arrive(*swaps)
         copies = []
         for d in (2, 1, 3, 0):
             mine, theirs = tokens_of(own, mod4(zl + d)), tokens_of(recv, mod4(zl + d))
-            mine[...] = mine[...] + theirs[...]
-            if d > 0:
-                copies.append(send(mine, zrecv.at[d - 1], dev(dzl=d)))
+            total = mine[...] + theirs[...]
+            if d == 0:
+                mine[...] = total
+            else:
+                for i, third in enumerate(pack(total)):
+                    zsend[d - 1, :, i * 256 : (i + 1) * 256] = third
+                copies.append(send(zsend.at[d - 1], zrecv.at[d - 1], dev(dzl=d)))
         return copies
 
-    te.y_forward("prev", prev, 0)
-    te.y_forward("next", nxt, 1)
-    at_2 = x_forward(at_1, at_buf)
+    def teacher_part(out, slot, zi, first):
+        a = at_buf[slot, :, pl.ds(pl.multiple_of(zi * 512, 512), 512)]
+        b = bt_buf[pl.ds(zi * 4, 4)].reshape(512, 512)
+        part = jnp.dot(a, b, preferred_element_type=F32)
+        out[...] = part if first else out[...] + part
+
+    def teacher_parts(zi, first):
+        for k in range(2):
+            teacher_part(ct_send.at[k], (1 - c) * 2 + k, zi, first)
+            teacher_part(ct_own.at[k], c * 2 + k, zi, first)
+
     arrive(te.zs[1, 1])
     te.y_start("prev", prev, 1)
     arrive(te.zs[3, 0])
     te.y_start("next", nxt, 0)
+    own_at.wait()
+    arrive(*at_2)
+    arrive(*te.last[:4])
+    teacher_parts(zh, True)
     arrive(te.zf[0])
     te.y_start("far", far, 0)
     arrive(te.zf[1])
     te.y_start("far", far, 1)
-    cs_z = scatter_z(cs_swap, cs_own, cs_recv, zs_recv)
+    cs_z = scatter_z(cs_swap, cs_own, cs_recv, zs_send, zs_recv)
     te.y_forward("prev", prev, 1)
     te.y_forward("next", nxt, 0)
     te.y_forward("far", far, 0)
     te.y_forward("far", far, 1)
-    arrive(*te.last)
-    own_at.wait()
-    arrive(*at_2)
-
-    def teacher_b(cols):
-        return bt_buf[:, :, cols].reshape(2048, 256)
-
-    ct_swap = both_cores(at_buf, teacher_b, ct_send, ct_recv, ct_own)
-    ct_z = scatter_z(ct_swap, ct_own, ct_recv, zt_recv)
+    arrive(*te.last[4:12])
+    teacher_parts(prev, False)
+    teacher_parts(nxt, False)
+    arrive(*te.last[12:])
+
+    ct_swap = []
+    for k in range(2):
+        teacher_part(ct_send.at[k], (1 - c) * 2 + k, far, False)
+        ct_swap.append(send(ct_send.at[k], ct_recv.at[k], dev(dc=1)))
+    for k in range(2):
+        teacher_part(ct_own.at[k], c * 2 + k, far, False)
+    ct_z = scatter_z(ct_swap, ct_own, ct_recv, zt_send, zt_recv)
+    drain()
 
     def scaled(own, zrecv):
-        return (tokens_of(own, zl)[...] + zrecv[0] + zrecv[1] + zrecv[2]) * 0.5
+        return (tokens_of(own, zl)[...] + sum(unpack(zrecv.at[k]) for k in range(3))) * 0.5
 
     arrive(*cs_z)
     s = scaled(cs_own, zs_recv)
@@ -476,8 +512,7 @@
             send(x_send.at[v, mod4(x + d)], gw_vmem.at[:, cols], dev(dx=d))
             for d in (2, 1, 3)
         ]
-    for copy in started:
-        copy.wait_send()
+    drain()
     arrive(*x_c)
     outs.append(write_out(gw_vmem, gw_out, 8))
     for copy in outs:
@@ -528,8 +563,10 @@
             pltpu.VMEM((2, 128, 512), F32),
             pltpu.VMEM((2, 128, 512), F32),
             pltpu.VMEM((2, 128, 512), F32),
-            pltpu.VMEM((3, 64, 512), F32),
-            pltpu.VMEM((3, 64, 512), F32),
+            pltpu.VMEM((3, 64, 768), BF16),
+            pltpu.VMEM((3, 64, 768), BF16),
+            pltpu.VMEM((3, 64, 768), BF16),
+            pltpu.VMEM((3, 64, 768), BF16),
             pltpu.VMEM((4, 8, 128), F32),
             pltpu.VMEM((2, 8, 64, 256), BF16),
             pltpu.VMEM((8, 8, 128), F32),

time: 106 us -> 104 us (0.981); the launches traced: 106 us -> 102 us
  Pallas kernels: 105 us -> 101 us
    pallas_call x1, Pallas kernels: 103 us -> 99.4 us  [body(): pl.pallas_call(distill_kernel, out_shape=out_shape, in_specs=[hbm] * 6, o...]
where the time goes in v4:
time: 104 us; the launch traced here: 102 us
  Pallas kernels  101 us (97%)
    pallas_call x1, Pallas kernels, body(): pl.pallas_call(distill_kernel, out_shape=out_shape, in_specs=[hbm] * 6, o...  99.4 us

profile of v4, /device:TPU:1, one launch (start us, length us, event | category | flops | bytes accessed | tf_op | source)
XLA Modules:
  0.0 101.8 jit_solution(5755294324421984218)
XLA Ops:
  0.6 99.4 %shard_map.85 = (f32[1,128]{1,0:T(1,128)}, f32[8,2048]{1,0:T(8,128)}, f32[128,512]{1,0:T(8,128)}) custom-call(bf16[128,2048]{1,0:T(8,128)(2,1)} %at_hbm.1, bf16[32,2048]{1,0:T(8,128)(2,1)} %bt_hbm.1, bf16[128,512]{1,0:T(8,128)(2,1)} %as_hbm.1, bf16[8,2048]{1,0:T(8,128)(2,1)} %sh_hbm.1, f32[1,128]{1,0:T(1,128)} %bitcast.3, f32[1,128]{1,0:T(1,128)} %bitcast.4), custom_call_target="tpu_custom_call" | custom-call | tf_op jit(solution)/shard_map/pallas_call | solution.py:542
  100.1 1.7 %shard_map.86 = (f32[1,128]{1,0:T(1,128)}, f32[8,2048]{1,0:T(8,128)}, f32[128,512]{1,0:T(8,128)}) custom-call(f32[1,128]{1,0:T(1,128)} %get-tuple-element.9.kl_in, f32[8,2048]{1,0:T(8,128)} %get-tuple-element.10.gw_in, f32[128,512]{1,0:T(8,128)} %get-tuple-element.11.gh_in), custom_call_target="tpu_custom_call" | custom-call | tf_op jit(solution)/shard_map/pallas_call | solution.py:601

commit v5 on v4

--- a/solution.py
+++ b/solution.py
@@ -43,8 +43,6 @@
     cs_send,
     cs_recv,
     cs_own,
-    zt_send,
-    zs_send,
     zt_recv,
     zs_recv,
     stat_buf,
@@ -211,46 +209,39 @@
             self.last.append(self.ys[name, h, 4 - d])
 
     prev, nxt, far = mod4(zh - 1), mod4(zh + 1), mod4(zh + 2)
-    st, te = Head(bs_buf, 32), Head(bt_buf, 64)
+    te = Head(bt_buf, 64)
 
     as_1 = x_start(as_hbm, as_buf)
     at_1 = x_start(at_hbm, at_buf)
 
+    def y_direct(zi):
+        ref = bs_buf.at[zi * 4 + y]
+        return [send(ref, ref, dev(dy=d)) for d in (1, 3, 2)]
+
     arrive(*bs_a2a)
-    st.z_start(order)
-    st.y_start("own", zh, 0)
-    st.y_start("own", zh, 1)
+    st_z = [send(bs_buf.at[piece], bs_buf.at[piece], dev(dzh=d)) for d in (1, 3)]
+    st_y = y_direct(zh)
     own_bt.wait()
     arrive(*bt_a2a)
     te.z_start(order[:2])
     te.y_start("own", zh, 0)
     te.y_start("own", zh, 1)
-
-    st.z_forward()
+    as_2 = x_forward(as_1, as_buf)
+    arrive(st_z[0])
+    st_f = [pass_on(bs_buf, prev * 4 + y, 0, 32, dev(dzh=1))]
+    arrive(st_z[1])
+    st_f.append(pass_on(bs_buf, nxt * 4 + y, 1, 32, dev(dzh=3)))
     te.z_start(order[2:])
-    st.y_start("prev", prev, 0)
-    st.y_start("next", nxt, 1)
-    as_2 = x_forward(as_1, as_buf)
-    st.y_forward("own", zh, 0)
-    st.y_forward("own", zh, 1)
-    arrive(st.zs[1, 1])
-    st.y_start("prev", prev, 1)
-    arrive(st.zs[3, 0])
-    st.y_start("next", nxt, 0)
-    st.y_forward("prev", prev, 0)
-    st.y_forward("next", nxt, 1)
+    st_y += y_direct(prev)
+    st_y += y_direct(nxt)
     te.y_forward("own", zh, 0)
     te.y_forward("own", zh, 1)
-    st.y_forward("prev", prev, 1)
-    st.y_forward("next", nxt, 0)
+    arrive(*st_f)
+    st_y += y_direct(far)
     at_2 = x_forward(at_1, at_buf)
     te.z_forward()
     te.y_start("prev", prev, 0)
     te.y_start("next", nxt, 1)
-    arrive(st.zf[0])
-    st.y_start("far", far, 0)
-    arrive(st.zf[1])
-    st.y_start("far", far, 1)
 
     own_as.wait()
     arrive(*as_2)
@@ -266,11 +257,9 @@
 
     lax.fori_loop(0, 4, turn, 0)
 
-    st.y_forward("far", far, 0)
-    st.y_forward("far", far, 1)
     te.y_forward("prev", prev, 0)
     te.y_forward("next", nxt, 1)
-    arrive(*st.last)
+    arrive(*st_y)
     for i in range(16):
         tall = bs_buf[i].astype(F32).reshape(4, 2, 8, 256)
         rows = slice(i * 32, (i + 1) * 32)
@@ -290,39 +279,14 @@
     def tokens_of(ref, chip):
         return ref.at[lax.div(chip, 2), pl.ds(pl.multiple_of(lax.rem(chip, 2) * 64, 64), 64)]
 
-    def pack(v):
-        halves = []
-        for w in (v[:, :256], v[:, 256:]):
-            near = w.astype(BF16)
-            wide = near.astype(F32)
-            size = jnp.abs(wide)
-            fits = size > 1e-30
-            steps = (w - wide) * (1792.0 / jnp.where(fits, size, 1.0))
-            halves.append((near, jnp.round(jnp.where(fits, steps, 0.0))))
-        (n0, r0), (n1, r1) = halves
-        return n0, n1, (16.0 * r0 + r1).astype(BF16)
-
-    def unpack(ref):
-        both = ref[:, 512:].astype(F32)
-        r0 = jnp.round(both * 0.0625)
-        out = []
-        for i, r in enumerate((r0, both - 16.0 * r0)):
-            wide = ref[:, i * 256 : (i + 1) * 256].astype(F32)
-            out.append(wide + r * (jnp.abs(wide) * (1.0 / 1792.0)))
-        return jnp.concatenate(out, axis=1)
-
-    def scatter_z(swaps, own, recv, zsend, zrecv):
+    def scatter_z(swaps, own, recv, zrecv):
         arrive(*swaps)
         copies = []
         for d in (2, 1, 3, 0):
             mine, theirs = tokens_of(own, mod4(zl + d)), tokens_of(recv, mod4(zl + d))
-            total = mine[...] + theirs[...]
-            if d == 0:
-                mine[...] = total
-            else:
-                for i, third in enumerate(pack(total)):
-                    zsend[d - 1, :, i * 256 : (i + 1) * 256] = third
-                copies.append(send(zsend.at[d - 1], zrecv.at[d - 1], dev(dzl=d)))
+            mine[...] = mine[...] + theirs[...]
+            if d > 0:
+                copies.append(send(mine, zrecv.at[d - 1], dev(dzl=d)))
         return copies
 
     def teacher_part(out, slot, zi, first):
@@ -348,7 +312,7 @@
     te.y_start("far", far, 0)
     arrive(te.zf[1])
     te.y_start("far", far, 1)
-    cs_z = scatter_z(cs_swap, cs_own, cs_recv, zs_send, zs_recv)
+    cs_z = scatter_z(cs_swap, cs_own, cs_recv, zs_recv)
     te.y_forward("prev", prev, 1)
     te.y_forward("next", nxt, 0)
     te.y_forward("far", far, 0)
@@ -364,11 +328,11 @@
         ct_swap.append(send(ct_send.at[k], ct_recv.at[k], dev(dc=1)))
     for k in range(2):
         teacher_part(ct_own.at[k], c * 2 + k, far, False)
-    ct_z = scatter_z(ct_swap, ct_own, ct_recv, zt_send, zt_recv)
+    ct_z = scatter_z(ct_swap, ct_own, ct_recv, zt_recv)
     drain()
 
     def scaled(own, zrecv):
-        return (tokens_of(own, zl)[...] + sum(unpack(zrecv.at[k]) for k in range(3))) * 0.5
+        return (tokens_of(own, zl)[...] + zrecv[0] + zrecv[1] + zrecv[2]) * 0.5
 
     arrive(*cs_z)
     s = scaled(cs_own, zs_recv)
@@ -563,10 +527,8 @@
             pltpu.VMEM((2, 128, 512), F32),
             pltpu.VMEM((2, 128, 512), F32),
             pltpu.VMEM((2, 128, 512), F32),
-            pltpu.VMEM((3, 64, 768), BF16),
-            pltpu.VMEM((3, 64, 768), BF16),
-            pltpu.VMEM((3, 64, 768), BF16),
-            pltpu.VMEM((3, 64, 768), BF16),
+            pltpu.VMEM((3, 64, 512), F32),
+            pltpu.VMEM((3, 64, 512), F32),
             pltpu.VMEM((4, 8, 128), F32),
             pltpu.VMEM((2, 8, 64, 256), BF16),
             pltpu.VMEM((8, 8, 128), F32),

time: 104 us -> 102 us (0.981)
  Pallas kernels: 101 us -> 99.6 us
    pallas_call x1, Pallas kernels: 99.4 us -> 97.9 us  [body(): pl.pallas_call(distill_kernel, out_shape=out_shape, in_specs=[hbm] * 6, o...]
where the time goes in v5:
time: 102 us; the launch traced here: 100 us
  Pallas kernels  99.6 us (98%)
    pallas_call x1, Pallas kernels, body(): pl.pallas_call(distill_kernel, out_shape=out_shape, in_specs=[hbm] * 6, o...  97.9 us

profile of v5, /device:TPU:1, one launch (start us, length us, event | category | flops | bytes accessed | tf_op | source)
XLA Modules:
  0.0 100.2 jit_solution(1188315182137993934)
XLA Ops:
  0.6 97.9 %shard_map.85 = (f32[1,128]{1,0:T(1,128)}, f32[8,2048]{1,0:T(8,128)}, f32[128,512]{1,0:T(8,128)}) custom-call(bf16[128,2048]{1,0:T(8,128)(2,1)} %at_hbm.1, bf16[32,2048]{1,0:T(8,128)(2,1)} %bt_hbm.1, bf16[128,512]{1,0:T(8,128)(2,1)} %as_hbm.1, bf16[8,2048]{1,0:T(8,128)(2,1)} %sh_hbm.1, f32[1,128]{1,0:T(1,128)} %bitcast.3, f32[1,128]{1,0:T(1,128)} %bitcast.4), custom_call_target="tpu_custom_call" | custom-call | tf_op jit(solution)/shard_map/pallas_call | solution.py:506
  98.5 1.7 %shard_map.86 = (f32[1,128]{1,0:T(1,128)}, f32[8,2048]{1,0:T(8,128)}, f32[128,512]{1,0:T(8,128)}) custom-call(f32[1,128]{1,0:T(1,128)} %get-tuple-element.9.kl_in, f32[8,2048]{1,0:T(8,128)} %get-tuple-element.10.gw_in, f32[128,512]{1,0:T(8,128)} %get-tuple-element.11.gh_in), custom_call_target="tpu_custom_call" | custom-call | tf_op jit(solution)/shard_map/pallas_call | solution.py:563

commit v6 on v5

--- a/solution.py
+++ b/solution.py
@@ -8,7 +8,7 @@
 MESH = pl.DeviceIdType.MESH
 F32 = jnp.float32
 BF16 = jnp.bfloat16
-N_COPY = 144
+N_COPY = 176
 
 
 def mod4(v):
@@ -189,11 +189,25 @@
                 self.zs[d, h] = pass_on(self.buf, piece, h, self.rows, dev(dzh=d))
 
         def z_forward(self):
-            arrive(self.zs[1, 0])
-            a = pass_on(self.buf, prev * 4 + y, 0, self.rows, dev(dzh=1))
-            arrive(self.zs[3, 1])
-            b = pass_on(self.buf, nxt * 4 + y, 1, self.rows, dev(dzh=3))
-            self.zf = (a, b)
+            self.zf = {}
+            for d, h, i in ((1, 0, prev * 4 + y), (3, 1, nxt * 4 + y)):
+                arrive(self.zs[d, h])
+                for k in (h * 2, h * 2 + 1):
+                    self.zf[k] = pass_on(self.buf, i, k, self.rows // 2, dev(dzh=d))
+
+        def far_start(self, k):
+            arrive(self.zf[k])
+            for d in (1, 3):
+                self.ys["far", k, d] = pass_on(
+                    self.buf, far * 4 + y, k, self.rows // 2, dev(dy=d)
+                )
+
+        def far_forward(self, k):
+            d = 1 if k < 2 else 3
+            arrive(self.ys["far", k, d])
+            i = far * 4 + mod4(y - 1 if k < 2 else y + 1)
+            self.last.append(pass_on(self.buf, i, k, self.rows // 2, dev(dy=d)))
+            self.last.append(self.ys["far", k, 4 - d])
 
         def y_start(self, name, zi, h):
             for d in (1, 3):
@@ -259,6 +273,10 @@
 
     te.y_forward("prev", prev, 0)
     te.y_forward("next", nxt, 1)
+    arrive(te.zs[1, 1])
+    te.y_start("prev", prev, 1)
+    arrive(te.zs[3, 0])
+    te.y_start("next", nxt, 0)
     arrive(*st_y)
     for i in range(16):
         tall = bs_buf[i].astype(F32).reshape(4, 2, 8, 256)
@@ -300,23 +318,17 @@
             teacher_part(ct_send.at[k], (1 - c) * 2 + k, zi, first)
             teacher_part(ct_own.at[k], c * 2 + k, zi, first)
 
-    arrive(te.zs[1, 1])
-    te.y_start("prev", prev, 1)
-    arrive(te.zs[3, 0])
-    te.y_start("next", nxt, 0)
+    cs_z = scatter_z(cs_swap, cs_own, cs_recv, zs_recv)
     own_at.wait()
     arrive(*at_2)
     arrive(*te.last[:4])
     teacher_parts(zh, True)
-    arrive(te.zf[0])
-    te.y_start("far", far, 0)
-    arrive(te.zf[1])
-    te.y_start("far", far, 1)
-    cs_z = scatter_z(cs_swap, cs_own, cs_recv, zs_recv)
+    for k in (0, 2, 1, 3):
+        te.far_start(k)
     te.y_forward("prev", prev, 1)
     te.y_forward("next", nxt, 0)
-    te.y_forward("far", far, 0)
-    te.y_forward("far", far, 1)
+    for k in (0, 2, 1, 3):
+        te.far_forward(k)
     arrive(*te.last[4:12])
     teacher_parts(prev, False)
     teacher_parts(nxt, False)

time: 102 us -> 102 us (level); the launches traced: 100 us -> 102 us
  Pallas kernels: 99.6 us -> 101 us
    pallas_call x1, Pallas kernels: 97.9 us -> 99.7 us  [body(): pl.pallas_call(distill_kernel, out_shape=out_shape, in_specs=[hbm] * 6, o...]
where the time goes in v6:
time: 102 us
  Pallas kernels  101 us (99%)
    pallas_call x1, Pallas kernels, body(): pl.pallas_call(distill_kernel, out_shape=out_shape, in_specs=[hbm] * 6, o...  99.7 us

profile of v6, /device:TPU:1, one launch (start us, length us, event | category | flops | bytes accessed | tf_op | source)
XLA Modules:
  0.0 102.0 jit_solution(11960449416685410998)
XLA Ops:
  0.6 99.7 %shard_map.85 = (f32[1,128]{1,0:T(1,128)}, f32[8,2048]{1,0:T(8,128)}, f32[128,512]{1,0:T(8,128)}) custom-call(bf16[128,2048]{1,0:T(8,128)(2,1)} %at_hbm.1, bf16[32,2048]{1,0:T(8,128)(2,1)} %bt_hbm.1, bf16[128,512]{1,0:T(8,128)(2,1)} %as_hbm.1, bf16[8,2048]{1,0:T(8,128)(2,1)} %sh_hbm.1, f32[1,128]{1,0:T(1,128)} %bitcast.3, f32[1,128]{1,0:T(1,128)} %bitcast.4), custom_call_target="tpu_custom_call" | custom-call | tf_op jit(solution)/shard_map/pallas_call | solution.py:518
  100.3 1.7 %shard_map.86 = (f32[1,128]{1,0:T(1,128)}, f32[8,2048]{1,0:T(8,128)}, f32[128,512]{1,0:T(8,128)}) custom-call(f32[1,128]{1,0:T(1,128)} %get-tuple-element.9.kl_in, f32[8,2048]{1,0:T(8,128)} %get-tuple-element.10.gw_in, f32[128,512]{1,0:T(8,128)} %get-tuple-element.11.gh_in), custom_call_target="tpu_custom_call" | custom-call | tf_op jit(solution)/shard_map/pallas_call | solution.py:575
